TPU v7x, 32 devices: a whole 2x2x4 slice. The times are simulated.
32 devices in a mesh: rep: 2 (over x), fsdp: 16 (over z, y, core).
Axes of the slice: x: 2, y: 2, z: 4, core: 2. Of those that a mesh axis runs over, the one named last changes fastest.
Arguments:
- hidden: bfloat16 [2, 4096, 256], P('rep', 'fsdp'), may hold values from -6 to 6
- global_w: float32 [256, 5120], P('fsdp'), may hold values from -0.375 to 0.375
- momentum: float32 [256, 5120], P('fsdp'), may hold values from -0.375 to 0.375
- inner: float32 [2, 256, 5120], P('rep', 'fsdp'), may hold values from -0.375 to 0.375
Outputs:
- global_new: float32 [256, 5120], P('fsdp')
- momentum_new: float32 [256, 5120], P('fsdp')
- projected: bfloat16 [2, 4096, 5120], P('rep', 'fsdp')
All inputs are finite; a program needn't handle non-finite values.
Results may differ from a plain program's by a relative error of at most 0.0049.
Values may be sent and summed in bfloat16 or wider, within the bound.
A program may use at most 64 MiB of HBM per device.

v0:
```python
import jax
import jax.numpy as jnp
from jax import lax
from jax.sharding import PartitionSpec as P


def outer_step(weights, moment, drift):
    moment_new = 0.9 * moment + drift
    return (weights - 0.7 * (drift + 0.9 * moment_new), moment_new)


def shards(hidden, global_w, momentum, inner):
    replicas = lax.axis_size("rep")
    own_inner = inner[0]
    local_drift = global_w - own_inner
    share = lax.psum_scatter(local_drift, "rep", scatter_dimension=1, tiled=True)
    width = share.shape[1]
    offset = lax.axis_index("rep") * width
    weight_part = lax.dynamic_slice_in_dim(global_w, offset, width, 1)
    moment_part = lax.dynamic_slice_in_dim(momentum, offset, width, 1)
    new_part, moment_done = outer_step(weight_part, moment_part, share / replicas)
    global_new, momentum_new = (
        lax.all_gather(new_part, "rep", axis=1, tiled=True),
        lax.all_gather(moment_done, "rep", axis=1, tiled=True),
    )
    blended = (0.5 * own_inner + 0.5 * global_new).astype(jnp.bfloat16)
    activations = hidden[0]
    result = jnp.dot(
        activations,
        lax.all_gather(blended, "fsdp", axis=0, tiled=True),
        preferred_element_type=jnp.float32,
    )
    return (global_new, momentum_new, result.astype(jnp.bfloat16)[None])


def solution(mesh):
    in_specs = (P("rep", "fsdp", None), P("fsdp", None), P("fsdp", None), P("rep", "fsdp", None))
    out_specs = (P("fsdp", None), P("fsdp", None), P("rep", "fsdp", None))
    return jax.shard_map(shards, mesh=mesh, in_specs=in_specs, out_specs=out_specs, check_vma=False)
```

profile of v0, /device:TPU:1, one launch (start us, length us, event | category | flops | bytes accessed | tf_op | source)
XLA Modules:
  0.0 91.3 jit_solution(11007562072758369402)
XLA Ops:
  7.2 0.0 copy-start
  7.2 0.0 copy-start.1
  7.2 0.0 reduce-scatter.2.cloned.1.call-start
  7.2 1.9 %bitcast_subtract_fusion = f32[16,5120]{1,0:T(8,128)} fusion(f32[16,5120]{1,0:T(8,128)} %param.5, f32[1,16,5120]{2,1,0:T(8,128)} %param.7), kind=kLoop, calls=%fused_computation.3 | loop fusion | flops 81920 | bytes 983040 | tf_op jit(solution)/shard_map/sub | solution.py:15
  9.1 0.0 reduce-scatter.2.cloned.1.call-update
  9.2 0.0 all-gather.2.cloned.1.call-start
  9.2 16.1 %reduce-scatter.2.cloned.1.call-done = f32[16,2560]{1,0:T(8,128)} async-done(((f32[16,5120]{1,0:T(8,128)}), f32[16,2560]{1,0:T(8,128)}) %reduce-scatter.2.cloned.1.call-update) | async-done | bytes 163856 | tf_op jit(solution)/shard_map/reduce_scatter | solution.py:16
  25.3 1.1 %multiply_add_fusion = (f32[16,2560]{1,0:T(8,128)S(1)}, f32[16,2560]{1,0:T(8,128)S(1)}) fusion(f32[16,5120]{1,0:T(8,128)} %param.6, s32[]{:T(128)S(6)} %select_n.4, f32[16,2560]{1,0:T(8,128)} %reduce-scatter.2.cloned.1.call-done, f32[16,5120]{1,0:T(8,128)} %param.5), kind=kLoop, calls=%fused_computation.7 | loop fusion | flops 286720 | bytes 819204 | tf_op jit(solution)/shard_map/add | solution.py:8
  26.5 5.7 %all_gather.9 = f32[16,5120]{1,0:T(8,128)S(1)} all-gather(f32[16,2560]{1,0:T(8,128)S(1)} %get-tuple-element.7), channel_id=1, replica_groups=mesh['rep'=2,'fsdp'=16] {'rep'}, dimensions={1}, use_global_device_ids=true | all-gather | bytes 491520 | tf_op jit(solution)/shard_map/all_gather | solution.py:23
  32.2 0.0 copy-done.1
  32.2 0.7 fusion.2
  32.9 0.0 all-gather.2.cloned.1.call-update
  32.9 4.8 %all_gather.10 = f32[16,5120]{1,0:T(8,128)S(1)} all-gather(f32[16,2560]{1,0:T(8,128)S(1)} %get-tuple-element.6), channel_id=1, replica_groups=mesh['rep'=2,'fsdp'=16] {'rep'}, dimensions={1}, use_global_device_ids=true | all-gather | bytes 491520 | tf_op jit(solution)/shard_map/all_gather | solution.py:24
  37.8 39.8 %all-gather.2.cloned.1.call-done = bf16[256,5120]{1,0:T(8,128)(2,1)} async-done(((bf16[16,5120]{1,0:T(8,128)(2,1)}), bf16[256,5120]{1,0:T(8,128)(2,1)}) %all-gather.2.cloned.1.call-update) | async-done | bytes 2621456 | tf_op jit(solution)/shard_map/all_gather | solution.py:30
  77.6 0.0 copy-done
  77.6 2.6 %fusion = bf16[1,256,5120]{1,2,0:T(8,128)(2,1)S(1)} fusion(bf16[256,5120]{1,0:T(8,128)(2,1)} %all-gather.2.cloned.1.call-done, bf16[1,256,256]{2,1,0:T(8,128)(2,1)S(1)} %copy-done), kind=kOutput, calls=%fused_computation.1 | convolution fusion | flops 672399360 | bytes 5373952 | tf_op jit(solution)/shard_map/dot_general | solution.py:28
  80.2 2.8 %copy.7 = bf16[1,256,5120]{2,1,0:T(8,128)(2,1)} copy(bf16[1,256,5120]{1,2,0:T(8,128)(2,1)S(1)} %fusion) | data formatting | bytes 5242880
  83.0 0.7 copy.10
  83.7 0.7 copy.11
Async XLA Ops:
  7.2 70.4 %copy-start = (bf16[1,256,256]{2,1,0:T(8,128)(2,1)S(1)}, bf16[1,256,256]{2,1,0:T(8,128)(2,1)}, u32[]{:S(2)}) copy-start(bf16[1,256,256]{2,1,0:T(8,128)(2,1)} %param.4) | copy-start | bytes 393220
  7.2 25.0 %copy-start.1 = (f32[1,16,5120]{2,1,0:T(8,128)S(1)}, f32[1,16,5120]{2,1,0:T(8,128)}, u32[]{:S(2)}) copy-start(f32[1,16,5120]{2,1,0:T(8,128)} %param.7) | copy-start | bytes 983044
  7.2 18.1 %reduce-scatter.2.cloned.1.call-start = ((), (), s32[]{:S(2)}) async-start(), calls=%async_computation.1 | async-start | bytes 491520 | tf_op jit(solution)/shard_map/reduce_scatter | solution.py:16
  9.2 68.4 %all-gather.2.cloned.1.call-start = ((), (), s32[]{:S(2)}) async-start(), calls=%async_computation.2 | async-start | bytes 2785280 | tf_op jit(solution)/shard_map/all_gather | solution.py:30
Sparse Core Ops, SparseCore 0:
  10.8 14.4 reduce-scatter.1
  33.0 44.4 all-gather.1
where the time goes:
time: 91.7 us; the launch traced here: 91.3 us
  waiting for transfers between devices  56 us (61%)
  between operations  14.1 us (15%)
  blocking collectives  10.6 us (12%)
  local copies, waits for them, and re-layouts  4.24 us (5%)
  other arithmetic  3.71 us (4%)
  matrix products  2.64 us (3%)
    all_gather x1, waiting for transfers between devices, shards(): lax.all_gather(blended, 'fsdp', axis=0, tiled=True)  39.8 us
    reduce_scatter x1, waiting for transfers between devices, shards(): lax.psum_scatter(local_drift, 'rep', scatter_dimension=1, tiled=True)  16.1 us
    all_gather x1, blocking collectives, shards(): lax.all_gather(new_part, 'rep', axis=1, tiled=True)  5.74 us
    all_gather x1, blocking collectives, shards(): lax.all_gather(moment_done, 'rep', axis=1, tiled=True)  4.85 us
    unnamed x7, local copies, waits for them, and re-layouts  4.24 us
    dot_general x1, matrix products, shards(): jnp.dot(activations, lax.all_gather(blended, 'fsdp', axis=0, tiled=True),...  2.64 us
    sub x1, other arithmetic, shards(): local_drift = global_w - own_inner  1.9 us
  transfers between devices with their start and end apart: 2, of which 2 were waited for; matrix products, arithmetic and copies ran while one was open for 0% of the time, Pallas kernels for 0%

commit v1 on v0

v1 whole, which is shorter than its diff:
```python
import functools

import jax
import jax.numpy as jnp
from jax import lax
from jax.experimental import pallas as pl
from jax.experimental.pallas import tpu as pltpu
from jax.sharding import PartitionSpec as P

CHUNK = 1024
FAST_FIRST = 1


def split_line(devices):
    chips = devices // 2
    long = 1
    while long * long < chips:
        long *= 2
    return long, chips // long


def ways(size):
    if size == 1:
        return []
    return [0] if size == 2 else [-1, 1]


def step(x, s):
    return 1 - x if s == 0 else x + s


def source(x, s, hops):
    return 1 - x if s == 0 else x - s * hops


def inside(x, size):
    return jnp.logical_and(x >= 0, x < size)


def guarded(size, x, body):
    if size == 2:
        body()
    else:
        pl.when(inside(x, size))(body)


def kernel(
    replicas, devices,
    hidden_hbm, global_hbm, moment_hbm, inner_hbm,
    global_out, moment_out, projected_out,
    hidden, weights, moment, inner, drifts, gathered, result, new_w, new_m,
    load_sem, store_sem, rep_send, rep_recv, line_send, twin_send, line_recv, twin_recv,
):
    rows, width = weights.shape
    cols = CHUNK if width % CHUNK == 0 else width
    count = width // cols
    long, short = split_line(devices)
    rep = lax.axis_index("rep")
    me = lax.axis_index("fsdp")
    core = lax.rem(me, 2)
    chip = lax.div(me, 2)
    place = (lax.div(chip, short), lax.rem(chip, short))
    sizes = (long, short)

    def index(a, b, c):
        return (a * short + b) * 2 + c

    def device_along(axis, s):
        spot = list(place)
        spot[axis] = step(spot[axis], s)
        return index(spot[0], spot[1], core)

    twin = index(place[0], place[1], 1 - core)

    barrier = pltpu.get_barrier_semaphore()
    heard = jnp.int32(replicas)
    for other in range(1, replicas):
        pl.semaphore_signal(
            barrier, inc=1, device_id=(lax.rem(rep + other, replicas), me),
            device_id_type=pl.DeviceIdType.MESH,
        )
    pl.semaphore_signal(barrier, inc=1, device_id=(rep, twin), device_id_type=pl.DeviceIdType.MESH)
    for axis in range(2):
        for s in ways(sizes[axis]):
            def greet(axis=axis, s=s):
                pl.semaphore_signal(
                    barrier, inc=1, device_id=(rep, device_along(axis, s)),
                    device_id_type=pl.DeviceIdType.MESH,
                )
            spot = step(place[axis], s)
            guarded(sizes[axis], spot, greet)
            heard = heard + (1 if sizes[axis] == 2 else inside(spot, sizes[axis]).astype(jnp.int32))

    loads = [
        pltpu.make_async_copy(global_hbm, weights, load_sem.at[0]),
        pltpu.make_async_copy(inner_hbm.at[0], inner, load_sem.at[1]),
        pltpu.make_async_copy(moment_hbm, moment, load_sem.at[2]),
        pltpu.make_async_copy(hidden_hbm.at[0], hidden, load_sem.at[3]),
    ]
    for load in loads:
        load.start()
    loads[0].wait()
    loads[1].wait()
    drifts[rep] = (weights[...] - inner[...]).astype(jnp.bfloat16)
    pl.semaphore_wait(barrier, heard)

    def span(k):
        return pl.ds(k * cols, cols)

    for k in range(count):
        for other in range(1, replicas):
            part = drifts.at[rep, :, span(k)]
            pltpu.make_async_remote_copy(
                src_ref=part, dst_ref=part, send_sem=rep_send, recv_sem=rep_recv.at[k],
                device_id=(lax.rem(rep + other, replicas), me),
                device_id_type=pl.DeviceIdType.MESH,
            ).start()

    def slot(origin, k):
        return gathered.at[pl.ds(pl.multiple_of(origin * rows, rows), rows), span(k)]

    def fast(k):
        return 1 if k < FAST_FIRST else 0

    def send_line(origin, k, axis, s):
        def go():
            pltpu.make_async_remote_copy(
                src_ref=slot(origin, k), dst_ref=slot(origin, k),
                send_sem=line_send.at[fast(k), axis, 0 if s < 1 else 1],
                recv_sem=line_recv.at[origin, k],
                device_id=(rep, device_along(axis, s)), device_id_type=pl.DeviceIdType.MESH,
            ).start()
        guarded(sizes[axis], step(place[axis], s), go)

    def send_twin(origin, k):
        pltpu.make_async_remote_copy(
            src_ref=slot(origin, k), dst_ref=slot(origin, k),
            send_sem=twin_send, recv_sem=twin_recv.at[k],
            device_id=(rep, twin), device_id_type=pl.DeviceIdType.MESH,
        ).start()

    def await_line(origin, k):
        part = slot(origin, k)
        pltpu.make_async_copy(part, part, line_recv.at[origin, k]).wait()

    def origin_at(axis, x, y):
        return index(x, y, core) if axis == 0 else index(y, x, core)

    def own(k):
        part = drifts.at[0:replicas - 1, :, span(k)]
        pltpu.make_async_copy(part, part, rep_recv.at[k]).wait()
        total = drifts[0, :, span(k)].astype(jnp.float32)
        for other in range(1, replicas):
            total = total + drifts[other, :, span(k)].astype(jnp.float32)
        drift = total / replicas
        moved = 0.9 * moment[:, span(k)] + drift
        fresh = weights[:, span(k)] - 0.7 * (drift + 0.9 * moved)
        blended = (0.5 * inner[:, span(k)] + 0.5 * fresh).astype(jnp.bfloat16)
        gathered[pl.ds(pl.multiple_of(me * rows, rows), rows), span(k)] = blended
        first = fast(k)
        for axis in (first, 1 - first):
            for s in ways(sizes[axis]):
                send_line(me, k, axis, s)
        send_twin(me, k)
        new_m[:, span(k)] = moved
        new_w[:, span(k)] = fresh

    def first_line(k, hops):
        axis = fast(k)
        size = sizes[axis]
        if hops >= size:
            return
        for s in ways(size):
            x = source(place[axis], s, hops)
            def body(x=x, s=s):
                origin = origin_at(axis, x, place[1 - axis])
                await_line(origin, k)
                if s != 0:
                    send_line(origin, k, axis, s)
                for t in ways(sizes[1 - axis]):
                    send_line(origin, k, 1 - axis, t)
                send_twin(origin, k)
            guarded(size, x, body)

    def second_line(k, away, hops):
        axis = fast(k)
        size, other = sizes[axis], sizes[1 - axis]
        if away >= size or hops >= other:
            return
        sides = [0] if away == 0 else ([1] if size == 2 else [-away, away])
        for side in sides:
            x = place[axis] if away == 0 else (1 - place[axis] if size == 2 else place[axis] + side)
            def line(x=x):
                for s in ways(other):
                    y = source(place[1 - axis], s, hops)
                    def body(y=y, s=s):
                        origin = origin_at(axis, x, y)
                        await_line(origin, k)
                        if s != 0:
                            send_line(origin, k, 1 - axis, s)
                        send_twin(origin, k)
                    guarded(other, y, body)
            if away == 0:
                line()
            else:
                guarded(size, x, line)

    def multiply(k):
        part = gathered.at[0:devices // 2 * rows, span(k)]
        pltpu.make_async_copy(part, part, twin_recv.at[k]).wait()
        result[:, span(k)] = jnp.dot(
            hidden[...], gathered[:, span(k)], preferred_element_type=jnp.float32
        ).astype(jnp.bfloat16)
        pltpu.make_async_copy(
            result.at[:, span(k)], projected_out.at[0, :, span(k)], store_sem.at[2 + k]
        ).start()

    loads[2].wait()
    for k in range(count):
        own(k)
    stores = [
        pltpu.make_async_copy(new_w, global_out, store_sem.at[0]),
        pltpu.make_async_copy(new_m, moment_out, store_sem.at[1]),
    ]
    for store in stores:
        store.start()
    loads[3].wait()

    rounds = [[] for _ in range(2 * (long + short))]
    for k in range(count):
        axis = fast(k)
        for away in range(sizes[axis]):
            if away > 0:
                rounds[away].append((k, functools.partial(first_line, k, away)))
            for hops in range(1, sizes[1 - axis]):
                rounds[away + hops].append((k, functools.partial(second_line, k, away, hops)))
    last = [0] * count
    for number, events in enumerate(rounds):
        for k, _ in events:
            last[k] = number
    for number, events in enumerate(rounds):
        events.sort(key=lambda event: event[0])
        for place_in, (k, event) in enumerate(events):
            event()
            if number == last[k] and k not in [j for j, _ in events[place_in + 1:]]:
                multiply(k)

    def drain(sem, blocks, columns):
        part = gathered.at[0:blocks * rows, 0:columns]
        pltpu.make_async_copy(part, part, sem).wait()

    for other in range(1):
        part = drifts.at[0:replicas - 1]
        pltpu.make_async_copy(part, part, rep_send).wait()
    drain(twin_send, devices // 2, width)
    fast_columns = min(FAST_FIRST, count) * cols
    for kind, columns in ((0, width - fast_columns), (1, fast_columns)):
        if columns == 0:
            continue
        for axis in range(2):
            lines = 1 if axis == kind else sizes[1 - axis]
            size, x = sizes[axis], place[axis]
            for s in ways(size):
                sem = line_send.at[kind, axis, 0 if s < 1 else 1]
                if s == 0:
                    drain(sem, lines, columns)
                    continue
                for blocks in range(1, size):
                    at = blocks - 1 if s == 1 else size - blocks
                    pl.when(x == at)(functools.partial(drain, sem, blocks * lines, columns))
    for store in stores:
        store.wait()
    for k in range(count):
        pltpu.make_async_copy(
            result.at[:, span(k)], projected_out.at[0, :, span(k)], store_sem.at[2 + k]
        ).wait()


def shards(replicas, devices, hidden, global_w, momentum, inner):
    _, tokens, units = hidden.shape
    rows, width = global_w.shape
    count = width // CHUNK if width % CHUNK == 0 else 1
    f32, bf16 = jnp.float32, jnp.bfloat16
    dma = pltpu.SemaphoreType.DMA
    room = rows * width * (4 * 5 + 2 * replicas) + units * width * 2 + tokens * (width + units) * 2
    return pl.pallas_call(
        functools.partial(kernel, replicas, devices),
        out_shape=(
            jax.ShapeDtypeStruct((rows, width), f32),
            jax.ShapeDtypeStruct((rows, width), f32),
            jax.ShapeDtypeStruct((1, tokens, width), bf16),
        ),
        in_specs=[pl.BlockSpec(memory_space=pl.ANY)] * 4,
        out_specs=[pl.BlockSpec(memory_space=pl.ANY)] * 3,
        scratch_shapes=[
            pltpu.VMEM((tokens, units), bf16),
            pltpu.VMEM((rows, width), f32),
            pltpu.VMEM((rows, width), f32),
            pltpu.VMEM((rows, width), f32),
            pltpu.VMEM((replicas, rows, width), bf16),
            pltpu.VMEM((units, width), bf16),
            pltpu.VMEM((tokens, width), bf16),
            pltpu.VMEM((rows, width), f32),
            pltpu.VMEM((rows, width), f32),
            dma((4,)),
            dma((2 + count,)),
            dma,
            dma((count,)),
            dma((2, 2, 2)),
            dma,
            dma((devices, count)),
            dma((count,)),
        ],
        compiler_params=pltpu.CompilerParams(
            collective_id=0, has_side_effects=True, vmem_limit_bytes=room + (8 << 20)
        ),
        cost_estimate=pl.CostEstimate(
            flops=2 * tokens * units * width,
            bytes_accessed=rows * width * 20 + tokens * width * 2,
            transcendentals=0,
        ),
    )(hidden, global_w, momentum, inner)


def solution(mesh):
    in_specs = (P("rep", "fsdp", None), P("fsdp", None), P("fsdp", None), P("rep", "fsdp", None))
    out_specs = (P("fsdp", None), P("fsdp", None), P("rep", "fsdp", None))
    body = functools.partial(shards, mesh.shape["rep"], mesh.shape["fsdp"])
    return jax.shard_map(body, mesh=mesh, in_specs=in_specs, out_specs=out_specs, check_vma=False)
```

time: 91.7 us -> 37.8 us (0.41)
  waiting for transfers between devices: 56 us -> 0 us
  Pallas kernels: 0 us -> 30.1 us
  between operations: 14.1 us -> 0.65 us
  blocking collectives: 10.6 us -> 0 us
  other arithmetic: 3.71 us -> 0 us
  matrix products: 2.64 us -> 0 us
  local copies, waits for them, and re-layouts: 4.24 us -> 6.76 us
    all_gather x1 -> x0, waiting for transfers between devices: 39.8 us -> none  [shards(): lax.all_gather(blended, 'fsdp', axis=0, tiled=True)]
    pallas_call x0 -> x1, Pallas kernels: none -> 30.1 us  [shards(): pl.pallas_call(functools.partial(kernel, replicas, devices), out_shape=(j...]
    reduce_scatter x1 -> x0, waiting for transfers between devices: 16.1 us -> none  [shards(): lax.psum_scatter(local_drift, 'rep', scatter_dimension=1, tiled=True)]
    all_gather x2 -> x0, blocking collectives: 10.6 us -> none  [the longest x1 5.74 us: shards(): lax.all_gather(new_part, 'rep', axis=1, tiled=True)]
    dot_general x1 -> x0, matrix products: 2.64 us -> none  [shards(): jnp.dot(activations, lax.all_gather(blended, 'fsdp', axis=0, tiled=True),...]
    unnamed x7 -> x11, local copies, waits for them, and re-layouts: 4.24 us -> 6.76 us
    sub x1 -> x0, other arithmetic: 1.9 us -> none  [shards(): local_drift = global_w - own_inner]
    add x1 -> x0, other arithmetic: 1.12 us -> none  [outer_step(): moment_new = 0.9 * moment + drift]
  transfers between devices with their start and end apart: 2 -> 0, of which waited for: 2 -> 0; matrix products, arithmetic and copies ran while one was open for 0% -> 0% of each run, Pallas kernels for 0% -> 0%
where the time goes in v1:
time: 37.8 us; the launch traced here: 37.5 us
  Pallas kernels  30.1 us (80%)
  local copies, waits for them, and re-layouts  6.76 us (18%)
  between operations  0.65 us (2%)
    pallas_call x1, Pallas kernels, shards(): pl.pallas_call(functools.partial(kernel, replicas, devices), out_shape=(j...  30.1 us
    unnamed x11, local copies, waits for them, and re-layouts  6.76 us

profile of v1, /device:TPU:1, one launch (start us, length us, event | category | flops | bytes accessed | tf_op | source)
XLA Modules:
  0.0 37.5 jit_solution(8893567670477997982)
XLA Ops:
  0.6 0.0 copy-start
  0.6 1.0 %copy-done = f32[16,5120]{1,0:T(8,128)S(1)} copy-done((f32[16,5120]{1,0:T(8,128)S(1)}, f32[16,5120]{1,0:T(8,128)}, u32[]{:S(2)}) %copy-start) | copy-done | bytes 327704
  1.6 0.0 copy-start.1
  1.6 1.0 %copy-done.1 = f32[16,5120]{1,0:T(8,128)S(1)} copy-done((f32[16,5120]{1,0:T(8,128)S(1)}, f32[16,5120]{1,0:T(8,128)}, u32[]{:S(2)}) %copy-start.1) | copy-done | bytes 327704
  2.6 0.0 copy-start.2
  2.6 1.0 %copy-done.2 = f32[1,16,5120]{2,1,0:T(8,128)S(1)} copy-done((f32[1,16,5120]{2,1,0:T(8,128)S(1)}, f32[1,16,5120]{2,1,0:T(8,128)}, u32[]{:S(2)}) %copy-start.2) | copy-done | bytes 327704
  3.6 0.0 copy-start.3
  3.6 0.9 %copy-done.3 = bf16[1,256,256]{2,1,0:T(8,128)(2,1)S(1)} copy-done((bf16[1,256,256]{2,1,0:T(8,128)(2,1)S(1)}, bf16[1,256,256]{2,1,0:T(8,128)(2,1)}, u32[]{:S(2)}) %copy-start.3) | copy-done | bytes 131096
  4.5 30.1 %shard_map.67 = (f32[16,5120]{1,0:T(8,128)S(1)}, f32[16,5120]{1,0:T(8,128)S(1)}, bf16[1,256,5120]{2,1,0:T(8,128)(2,1)S(1)}) custom-call(bf16[1,256,256]{2,1,0:T(8,128)(2,1)S(1)} %copy-done.3, f32[16,5120]{1,0:T(8,128)S(1)} %copy-done, f32[16,5120]{1,0:T(8,128)S(1)} %copy-done.1, f32[1,16,5120]{2,1,0:T(8,128)S(1)} %copy-done.2), custom_call_target="tpu_custom_call" | custom-call | flops 671088640 | bytes 4259840 | tf_op jit(solution)/shard_map/pallas_call | solution.py:286
  34.6 0.7 %copy.10 = f32[16,5120]{1,0:T(8,128)} copy(f32[16,5120]{1,0:T(8,128)S(1)} %get-tuple-element.6) | data formatting | bytes 655360
  35.3 0.7 %copy.11 = f32[16,5120]{1,0:T(8,128)} copy(f32[16,5120]{1,0:T(8,128)S(1)} %get-tuple-element.7) | data formatting | bytes 655360
  36.0 1.5 %copy.12 = bf16[1,256,5120]{2,1,0:T(8,128)(2,1)} copy(bf16[1,256,5120]{2,1,0:T(8,128)(2,1)S(1)} %get-tuple-element.8) | data formatting | bytes 5242880
Async XLA Ops:
  0.6 1.0 %copy-start = (f32[16,5120]{1,0:T(8,128)S(1)}, f32[16,5120]{1,0:T(8,128)}, u32[]{:S(2)}) copy-start(f32[16,5120]{1,0:T(8,128)} %global_hbm.1) | copy-start | bytes 983044
  1.6 1.0 %copy-start.1 = (f32[16,5120]{1,0:T(8,128)S(1)}, f32[16,5120]{1,0:T(8,128)}, u32[]{:S(2)}) copy-start(f32[16,5120]{1,0:T(8,128)} %moment_hbm.1) | copy-start | bytes 983044
  2.6 1.0 %copy-start.2 = (f32[1,16,5120]{2,1,0:T(8,128)S(1)}, f32[1,16,5120]{2,1,0:T(8,128)}, u32[]{:S(2)}) copy-start(f32[1,16,5120]{2,1,0:T(8,128)} %inner_hbm.1) | copy-start | bytes 983044
  3.6 0.9 %copy-start.3 = (bf16[1,256,256]{2,1,0:T(8,128)(2,1)S(1)}, bf16[1,256,256]{2,1,0:T(8,128)(2,1)}, u32[]{:S(2)}) copy-start(bf16[1,256,256]{2,1,0:T(8,128)(2,1)} %hidden_hbm.1) | copy-start | bytes 393220

commit v2 on v1

--- a/solution.py
+++ b/solution.py
@@ -7,8 +7,10 @@
 from jax.experimental.pallas import tpu as pltpu
 from jax.sharding import PartitionSpec as P
 
-CHUNK = 1024
-FAST_FIRST = 1
+CUTS = (1,)
+LAG = 0.0
+RELEASE = 0.0
+FAST = 0
 
 
 def split_line(devices):
@@ -44,16 +46,25 @@
         pl.when(inside(x, size))(body)
 
 
+def cut(width):
+    total, starts, widths = sum(CUTS), [], []
+    for number in range(len(CUTS)):
+        at, end = (width * sum(CUTS[:number + more]) // total // 128 * 128 for more in (0, 1))
+        starts.append(at)
+        widths.append((width if number + 1 == len(CUTS) else end) - at)
+    return starts, widths
+
+
 def kernel(
     replicas, devices,
     hidden_hbm, global_hbm, moment_hbm, inner_hbm,
-    global_out, moment_out, projected_out,
-    hidden, weights, moment, inner, drifts, gathered, result, new_w, new_m,
-    load_sem, store_sem, rep_send, rep_recv, line_send, twin_send, line_recv, twin_recv,
+    new_w, new_m, result,
+    hidden, weights, moment, inner, drifts, gathered,
+    load_sem, rep_send, rep_recv, line_send, twin_send, line_recv, twin_recv,
 ):
     rows, width = weights.shape
-    cols = CHUNK if width % CHUNK == 0 else width
-    count = width // cols
+    starts, widths = cut(width)
+    count = len(widths)
     long, short = split_line(devices)
     rep = lax.axis_index("rep")
     me = lax.axis_index("fsdp")
@@ -105,7 +116,7 @@
     pl.semaphore_wait(barrier, heard)
 
     def span(k):
-        return pl.ds(k * cols, cols)
+        return pl.ds(starts[k], widths[k])
 
     for k in range(count):
         for other in range(1, replicas):
@@ -120,7 +131,7 @@
         return gathered.at[pl.ds(pl.multiple_of(origin * rows, rows), rows), span(k)]
 
     def fast(k):
-        return 1 if k < FAST_FIRST else 0
+        return 1 if k >= count - FAST else 0
 
     def send_line(origin, k, axis, s):
         def go():
@@ -157,8 +168,7 @@
         fresh = weights[:, span(k)] - 0.7 * (drift + 0.9 * moved)
         blended = (0.5 * inner[:, span(k)] + 0.5 * fresh).astype(jnp.bfloat16)
         gathered[pl.ds(pl.multiple_of(me * rows, rows), rows), span(k)] = blended
-        first = fast(k)
-        for axis in (first, 1 - first):
+        for axis in ((1,) if fast(k) else (0, 1)):
             for s in ways(sizes[axis]):
                 send_line(me, k, axis, s)
         send_twin(me, k)
@@ -177,10 +187,16 @@
                 await_line(origin, k)
                 if s != 0:
                     send_line(origin, k, axis, s)
-                for t in ways(sizes[1 - axis]):
-                    send_line(origin, k, 1 - axis, t)
+                if axis == 0:
+                    for t in ways(sizes[1]):
+                        send_line(origin, k, 1, t)
                 send_twin(origin, k)
             guarded(size, x, body)
+
+    def release(k):
+        for y in range(short):
+            for s in ways(long):
+                send_line(index(place[0], y, core), k, 0, s)
 
     def second_line(k, away, hops):
         axis = fast(k)
@@ -211,39 +227,46 @@
         result[:, span(k)] = jnp.dot(
             hidden[...], gathered[:, span(k)], preferred_element_type=jnp.float32
         ).astype(jnp.bfloat16)
-        pltpu.make_async_copy(
-            result.at[:, span(k)], projected_out.at[0, :, span(k)], store_sem.at[2 + k]
-        ).start()
 
     loads[2].wait()
+
+    slow = count - FAST
+    ends = [(start + size) / width for start, size in zip(starts, widths)]
+    share = starts[slow] / width if FAST else 1.0
+    delay = 0.5
+    events = []
     for k in range(count):
-        own(k)
-    stores = [
-        pltpu.make_async_copy(new_w, global_out, store_sem.at[0]),
-        pltpu.make_async_copy(new_m, moment_out, store_sem.at[1]),
-    ]
-    for store in stores:
-        store.start()
-    loads[3].wait()
-
-    rounds = [[] for _ in range(2 * (long + short))]
-    for k in range(count):
-        axis = fast(k)
-        for away in range(sizes[axis]):
+        if fast(k):
+            part = ends[k] - share
+            events.append((part / 2, k, functools.partial(own, k)))
+            for hops in range(1, short):
+                events.append((part + delay * hops, k, functools.partial(first_line, k, hops)))
+            events.append((share * (long - 2) + part + RELEASE, k, functools.partial(release, k)))
+            for away in range(short):
+                for hops in range(1, long):
+                    at = share * (long - 1) + short * ((1 - share) * (hops - 1) + part) + delay
+                    events.append((at + 0.01 * away, k, functools.partial(second_line, k, away, hops)))
+            continue
+        part = ends[k]
+        events.append((1 - share + part, k, functools.partial(own, k)))
+        for away in range(long):
             if away > 0:
-                rounds[away].append((k, functools.partial(first_line, k, away)))
-            for hops in range(1, sizes[1 - axis]):
-                rounds[away + hops].append((k, functools.partial(second_line, k, away, hops)))
-    last = [0] * count
-    for number, events in enumerate(rounds):
-        for k, _ in events:
-            last[k] = number
-    for number, events in enumerate(rounds):
-        events.sort(key=lambda event: event[0])
-        for place_in, (k, event) in enumerate(events):
-            event()
-            if number == last[k] and k not in [j for j, _ in events[place_in + 1:]]:
-                multiply(k)
+                at = share * (away - 1) + part + delay
+                events.append((at, k, functools.partial(first_line, k, away)))
+            for hops in range(1, short):
+                at = 1 - share + share * (away + hops - 1) + part + delay * (1 if away == 0 else 2) + LAG
+                events.append((at, k, functools.partial(second_line, k, away, hops)))
+    events.sort(key=lambda event: event[0])
+    final = {k: number for number, (_, k, _) in enumerate(events)}
+    owns = count
+    for number, (_, k, event) in enumerate(events):
+        event()
+        if event.func is own:
+            owns -= 1
+            if owns == 0:
+                loads[3].wait()
+        if number == final[k]:
+            multiply(k)
 
     def drain(sem, blocks, columns):
         part = gathered.at[0:blocks * rows, 0:columns]
@@ -253,7 +276,7 @@
         part = drifts.at[0:replicas - 1]
         pltpu.make_async_copy(part, part, rep_send).wait()
     drain(twin_send, devices // 2, width)
-    fast_columns = min(FAST_FIRST, count) * cols
+    fast_columns = sum(widths[count - FAST:]) if FAST else 0
     for kind, columns in ((0, width - fast_columns), (1, fast_columns)):
         if columns == 0:
             continue
@@ -268,30 +291,27 @@
                 for blocks in range(1, size):
                     at = blocks - 1 if s == 1 else size - blocks
                     pl.when(x == at)(functools.partial(drain, sem, blocks * lines, columns))
-    for store in stores:
-        store.wait()
-    for k in range(count):
-        pltpu.make_async_copy(
-            result.at[:, span(k)], projected_out.at[0, :, span(k)], store_sem.at[2 + k]
-        ).wait()
 
 
 def shards(replicas, devices, hidden, global_w, momentum, inner):
     _, tokens, units = hidden.shape
     rows, width = global_w.shape
-    count = width // CHUNK if width % CHUNK == 0 else 1
+    count = len(CUTS)
     f32, bf16 = jnp.float32, jnp.bfloat16
     dma = pltpu.SemaphoreType.DMA
     room = rows * width * (4 * 5 + 2 * replicas) + units * width * 2 + tokens * (width + units) * 2
-    return pl.pallas_call(
+    hidden, global_w, momentum, inner = [
+        pltpu.with_memory_space_constraint(x, pltpu.HBM) for x in (hidden, global_w, momentum, inner)
+    ]
+    fresh, moved, product = pl.pallas_call(
         functools.partial(kernel, replicas, devices),
         out_shape=(
             jax.ShapeDtypeStruct((rows, width), f32),
             jax.ShapeDtypeStruct((rows, width), f32),
-            jax.ShapeDtypeStruct((1, tokens, width), bf16),
+            jax.ShapeDtypeStruct((tokens, width), bf16),
         ),
-        in_specs=[pl.BlockSpec(memory_space=pl.ANY)] * 4,
-        out_specs=[pl.BlockSpec(memory_space=pl.ANY)] * 3,
+        in_specs=[pl.BlockSpec(memory_space=pltpu.HBM)] * 4,
+        out_specs=[pl.BlockSpec(memory_space=pltpu.VMEM)] * 3,
         scratch_shapes=[
             pltpu.VMEM((tokens, units), bf16),
             pltpu.VMEM((rows, width), f32),
@@ -299,11 +319,7 @@
             pltpu.VMEM((rows, width), f32),
             pltpu.VMEM((replicas, rows, width), bf16),
             pltpu.VMEM((units, width), bf16),
-            pltpu.VMEM((tokens, width), bf16),
-            pltpu.VMEM((rows, width), f32),
-            pltpu.VMEM((rows, width), f32),
             dma((4,)),
-            dma((2 + count,)),
             dma,
             dma((count,)),
             dma((2, 2, 2)),
@@ -320,6 +336,29 @@
             transcendentals=0,
         ),
     )(hidden, global_w, momentum, inner)
+    fresh, moved, product = [
+        pltpu.with_memory_space_constraint(x, pltpu.VMEM) for x in (fresh, moved, product)
+    ]
+    outs = pl.pallas_call(
+        write_out,
+        out_shape=[jax.ShapeDtypeStruct(x.shape, x.dtype) for x in (fresh, moved, product)],
+        in_specs=[pl.BlockSpec(memory_space=pltpu.VMEM)] * 3,
+        out_specs=[pl.BlockSpec(memory_space=pl.ANY)] * 3,
+        scratch_shapes=[dma((3,))],
+    )(fresh, moved, product)
+    return outs[0], outs[1], outs[2][None]
+
+
+def write_out(*refs):
+    half = len(refs) // 2
+    copies = [
+        pltpu.make_async_copy(source_ref, target, refs[-1].at[number])
+        for number, (source_ref, target) in enumerate(zip(refs[:half], refs[half:-1]))
+    ]
+    for copy in copies:
+        copy.start()
+    for copy in copies:
+        copy.wait()
 
 
 def solution(mesh):

time: 37.8 us -> 32.8 us (0.87)
  local copies, waits for them, and re-layouts: 6.76 us -> 0 us
  Pallas kernels: 30.1 us -> 32.1 us
    unnamed x11 -> x0, local copies, waits for them, and re-layouts: 6.76 us -> none
    pallas_call x0 -> x1, Pallas kernels: none -> 1.74 us  [shards(): pl.pallas_call(write_out, out_shape=[jax.ShapeDtypeStruct(x.shape, x.dtyp...]
where the time goes in v2:
time: 32.8 us; the launch traced here: 32.7 us
  Pallas kernels  32.1 us (98%)
  between operations  0.64 us (2%)
    pallas_call x1, Pallas kernels, shards(): pl.pallas_call(functools.partial(kernel, replicas, devices), out_shape=(j...  30.3 us
    pallas_call x1, Pallas kernels, shards(): pl.pallas_call(write_out, out_shape=[jax.ShapeDtypeStruct(x.shape, x.dtyp...  1.74 us

profile of v2, /device:TPU:1, one launch (start us, length us, event | category | flops | bytes accessed | tf_op | source)
XLA Modules:
  0.0 32.7 jit_solution(7997039590956004837)
XLA Ops:
  0.6 30.3 %shard_map.67 = (f32[16,5120]{1,0:T(8,128)S(1)}, f32[16,5120]{1,0:T(8,128)S(1)}, bf16[256,5120]{1,0:T(8,128)(2,1)S(1)}) custom-call(bf16[1,256,256]{2,1,0:T(8,128)(2,1)} %hidden_hbm.1, f32[16,5120]{1,0:T(8,128)} %global_hbm.1, f32[16,5120]{1,0:T(8,128)} %moment_hbm.1, f32[1,16,5120]{2,1,0:T(8,128)} %inner_hbm.1), custom_call_target="tpu_custom_call" | custom-call | flops 671088640 | bytes 4259840 | tf_op jit(solution)/shard_map/pallas_call | solution.py:306
  31.0 1.7 %shard_map.68 = (f32[16,5120]{1,0:T(8,128)}, f32[16,5120]{1,0:T(8,128)}, bf16[256,5120]{1,0:T(8,128)(2,1)}) custom-call(f32[16,5120]{1,0:T(8,128)S(1)} %get-tuple-element.9.refs_0_, f32[16,5120]{1,0:T(8,128)S(1)} %get-tuple-element.10.refs_1_, bf16[256,5120]{1,0:T(8,128)(2,1)S(1)} %get-tuple-element.11.refs_2_), custom_call_target="tpu_custom_call" | custom-call | tf_op jit(solution)/shard_map/pallas_call | solution.py:342

commit v3 on v2

--- a/solution.py
+++ b/solution.py
@@ -8,6 +8,7 @@
 from jax.sharding import PartitionSpec as P
 
 CUTS = (1,)
+TILES = 5
 LAG = 0.0
 RELEASE = 0.0
 FAST = 0
@@ -58,8 +59,8 @@
 def kernel(
     replicas, devices,
     hidden_hbm, global_hbm, moment_hbm, inner_hbm,
-    new_w, new_m, result,
-    hidden, weights, moment, inner, drifts, gathered,
+    new_w, new_m, gathered, hidden,
+    weights, moment, inner, drifts,
     load_sem, rep_send, rep_recv, line_send, twin_send, line_recv, twin_recv,
 ):
     rows, width = weights.shape
@@ -221,12 +222,9 @@
             else:
                 guarded(size, x, line)
 
-    def multiply(k):
+    def complete(k):
         part = gathered.at[0:devices // 2 * rows, span(k)]
         pltpu.make_async_copy(part, part, twin_recv.at[k]).wait()
-        result[:, span(k)] = jnp.dot(
-            hidden[...], gathered[:, span(k)], preferred_element_type=jnp.float32
-        ).astype(jnp.bfloat16)
 
     loads[2].wait()
 
@@ -266,7 +264,7 @@
             if owns == 0:
                 loads[3].wait()
         if number == final[k]:
-            multiply(k)
+            complete(k)
 
     def drain(sem, blocks, columns):
         part = gathered.at[0:blocks * rows, 0:columns]
@@ -303,22 +301,21 @@
     hidden, global_w, momentum, inner = [
         pltpu.with_memory_space_constraint(x, pltpu.HBM) for x in (hidden, global_w, momentum, inner)
     ]
-    fresh, moved, product = pl.pallas_call(
+    held = pl.pallas_call(
         functools.partial(kernel, replicas, devices),
         out_shape=(
             jax.ShapeDtypeStruct((rows, width), f32),
             jax.ShapeDtypeStruct((rows, width), f32),
-            jax.ShapeDtypeStruct((tokens, width), bf16),
+            jax.ShapeDtypeStruct((units, width), bf16),
+            jax.ShapeDtypeStruct((tokens, units), bf16),
         ),
         in_specs=[pl.BlockSpec(memory_space=pltpu.HBM)] * 4,
-        out_specs=[pl.BlockSpec(memory_space=pltpu.VMEM)] * 3,
+        out_specs=[pl.BlockSpec(memory_space=pltpu.VMEM)] * 4,
         scratch_shapes=[
-            pltpu.VMEM((tokens, units), bf16),
             pltpu.VMEM((rows, width), f32),
             pltpu.VMEM((rows, width), f32),
             pltpu.VMEM((rows, width), f32),
             pltpu.VMEM((replicas, rows, width), bf16),
-            pltpu.VMEM((units, width), bf16),
             dma((4,)),
             dma,
             dma((count,)),
@@ -336,27 +333,39 @@
             transcendentals=0,
         ),
     )(hidden, global_w, momentum, inner)
-    fresh, moved, product = [
-        pltpu.with_memory_space_constraint(x, pltpu.VMEM) for x in (fresh, moved, product)
-    ]
+    held = [pltpu.with_memory_space_constraint(x, pltpu.VMEM) for x in held]
     outs = pl.pallas_call(
         write_out,
-        out_shape=[jax.ShapeDtypeStruct(x.shape, x.dtype) for x in (fresh, moved, product)],
-        in_specs=[pl.BlockSpec(memory_space=pltpu.VMEM)] * 3,
+        out_shape=(
+            jax.ShapeDtypeStruct((rows, width), f32),
+            jax.ShapeDtypeStruct((rows, width), f32),
+            jax.ShapeDtypeStruct((tokens, width), bf16),
+        ),
+        in_specs=[pl.BlockSpec(memory_space=pltpu.VMEM)] * 4,
         out_specs=[pl.BlockSpec(memory_space=pl.ANY)] * 3,
-        scratch_shapes=[dma((3,))],
-    )(fresh, moved, product)
+        scratch_shapes=[pltpu.VMEM((tokens, width), bf16), dma((2 + TILES,))],
+        compiler_params=pltpu.CompilerParams(vmem_limit_bytes=room + (8 << 20)),
+    )(*held)
     return outs[0], outs[1], outs[2][None]
 
 
-def write_out(*refs):
-    half = len(refs) // 2
+def write_out(new_w, new_m, gathered, hidden, global_out, moment_out, projected_out, result, sem):
     copies = [
-        pltpu.make_async_copy(source_ref, target, refs[-1].at[number])
-        for number, (source_ref, target) in enumerate(zip(refs[:half], refs[half:-1]))
+        pltpu.make_async_copy(new_w, global_out, sem.at[0]),
+        pltpu.make_async_copy(new_m, moment_out, sem.at[1]),
     ]
     for copy in copies:
         copy.start()
+    tile = gathered.shape[1] // TILES
+    for number in range(TILES):
+        span = pl.ds(number * tile, tile)
+        result[:, span] = jnp.dot(
+            hidden[...], gathered[:, span], preferred_element_type=jnp.float32
+        ).astype(jnp.bfloat16)
+        copies.append(
+            pltpu.make_async_copy(result.at[:, span], projected_out.at[:, span], sem.at[2 + number])
+        )
+        copies[-1].start()
     for copy in copies:
         copy.wait()
 

time: 32.8 us -> 32.2 us (0.982)
  Pallas kernels: 32.1 us -> 31.3 us
    pallas_call x1, Pallas kernels: 30.3 us -> 29.5 us  [shards(): pl.pallas_call(functools.partial(kernel, replicas, devices), out_shape=(j...]
where the time goes in v3:
time: 32.2 us; the launch traced here: 32 us
  Pallas kernels  31.3 us (97%)
  between operations  0.64 us (2%)
    pallas_call x1, Pallas kernels, shards(): pl.pallas_call(functools.partial(kernel, replicas, devices), out_shape=(j...  29.5 us
    pallas_call x1, Pallas kernels, shards(): pl.pallas_call(write_out, out_shape=(jax.ShapeDtypeStruct((rows, width),...  1.85 us

profile of v3, /device:TPU:1, one launch (start us, length us, event | category | flops | bytes accessed | tf_op | source)
XLA Modules:
  0.0 32.0 jit_solution(71071563333822186)
XLA Ops:
  0.6 29.5 %shard_map.67 = (f32[16,5120]{1,0:T(8,128)S(1)}, f32[16,5120]{1,0:T(8,128)S(1)}, bf16[256,5120]{1,0:T(8,128)(2,1)S(1)}, bf16[256,256]{1,0:T(8,128)(2,1)S(1)}) custom-call(bf16[1,256,256]{2,1,0:T(8,128)(2,1)} %hidden_hbm.1, f32[16,5120]{1,0:T(8,128)} %global_hbm.1, f32[16,5120]{1,0:T(8,128)} %moment_hbm.1, f32[1,16,5120]{2,1,0:T(8,128)} %inner_hbm.1), custom_call_target="tpu_custom_call" | custom-call | flops 671088640 | bytes 4259840 | tf_op jit(solution)/shard_map/pallas_call | solution.py:304
  30.1 1.9 %shard_map.68 = (f32[16,5120]{1,0:T(8,128)}, f32[16,5120]{1,0:T(8,128)}, bf16[256,5120]{1,0:T(8,128)(2,1)}) custom-call(f32[16,5120]{1,0:T(8,128)S(1)} %get-tuple-element.10.new_w, f32[16,5120]{1,0:T(8,128)S(1)} %get-tuple-element.11.new_m, bf16[256,5120]{1,0:T(8,128)(2,1)S(1)} %get-tuple-element.12.gathered, bf16[256,256]{1,0:T(8,128)(2,1)S(1)} %get-tuple-element.13.hidden), custom_call_target="tpu_custom_call" | custom-call | tf_op jit(solution)/shard_map/pallas_call | solution.py:337
